TPU v7x, 32 devices: a whole 2x2x4 slice. The times are simulated.
32 devices in a mesh: dp: 2 (over y), expert: 16 (over z, x, core).
Axes of the slice: x: 2, y: 2, z: 4, core: 2. Of those that a mesh axis runs over, the one named last changes fastest.
Arguments:
- tokens: bfloat16 [1024, 2048], P(('dp', 'expert')), may hold values from -6 to 6
- routes: int32 [1024, 8], P(('dp', 'expert')), may hold values from 0 to 15, all different within a row; in each aligned block of 32 rows (0 to 31, 32 to 63, ...) at most 32 rows name the same one
- cotangent: bfloat16 [1024, 2048], P(('dp', 'expert')), may hold values from -6 to 6
- router_weight: bfloat16 [2048, 16], replicated, may hold values from -0.375 to 0.375
- gate_weight: bfloat16 [16, 2048, 768], P('expert'), may hold values from -0.125 to 0.125
- up_weight: bfloat16 [16, 2048, 768], P('expert'), may hold values from -0.125 to 0.125
- down_weight: bfloat16 [16, 768, 2048], P('expert'), may hold values from -0.21875 to 0.21875
Outputs:
- layer_out: bfloat16 [1024, 2048], P(('dp', 'expert'))
- token_grad: bfloat16 [1024, 2048], P(('dp', 'expert'))
- gate_grad: bfloat16 [16, 2048, 768], P('expert', 'dp')
- up_grad: bfloat16 [16, 2048, 768], P('expert', 'dp')
- down_grad: bfloat16 [16, 768, 2048], P('expert', None, 'dp')
- router_grad: float32 [2048, 16], replicated
Inputs may be any that keep to these rules, and one draw needn't show every extreme that they name: `routes`: each row names 8 different experts. Among the 32 rows of one device no expert is named by more than 32 rows, and in some device's rows an expert is named by exactly 32 rows.
All inputs are finite; a program needn't handle non-finite values.
Results may differ from a plain program's by a relative error of at most 0.0061.
Values may be sent and summed in bfloat16 or wider, within the bound.
A program may use at most 128 MiB of HBM per device.

v0:
```python
import jax
import jax.numpy as jnp
from jax import lax
from jax.sharding import PartitionSpec as P


def silu_parts(gate_act):
    sigmoid_value = jax.nn.sigmoid(gate_act)
    act_value = gate_act * sigmoid_value
    act_slope = sigmoid_value * (1.0 + gate_act * (1.0 - sigmoid_value))
    return (act_value, act_slope)


def expert_forward(arrived, gate_weight, up_weight, down_weight):
    gate_act = jnp.einsum(
        "sjcd,jdf->sjcf", arrived, gate_weight, preferred_element_type=jnp.float32
    )
    up_act = jnp.einsum("sjcd,jdf->sjcf", arrived, up_weight, preferred_element_type=jnp.float32)
    act_value, act_slope = silu_parts(gate_act)
    hidden = (act_value * up_act).astype(jnp.bfloat16)
    expert_out = jnp.einsum(
        "sjcf,jfd->sjcd", hidden, down_weight, preferred_element_type=jnp.float32
    ).astype(jnp.bfloat16)
    return (expert_out, (up_act, act_value, act_slope, hidden))


def expert_backward(arrived_grads, stored, gate_weight, up_weight, down_weight):
    up_act, act_value, act_slope, hidden = stored
    hidden_grad = jnp.einsum(
        "sjcd,jfd->sjcf", arrived_grads, down_weight, preferred_element_type=jnp.float32
    )
    gate_part = (hidden_grad * up_act * act_slope).astype(jnp.bfloat16)
    up_part = (hidden_grad * act_value).astype(jnp.bfloat16)
    input_grad = (
        jnp.einsum("sjcf,jdf->sjcd", gate_part, gate_weight, preferred_element_type=jnp.float32)
        + jnp.einsum("sjcf,jdf->sjcd", up_part, up_weight, preferred_element_type=jnp.float32)
    ).astype(jnp.bfloat16)
    return (input_grad, gate_part, up_part)


def local(tokens, routes, cotangent, router_weight, gate_weight, up_weight, down_weight):
    tok_rows, top_count = routes.shape
    model_width = tokens.shape[1]
    expert_count = router_weight.shape[1]
    local_count = gate_weight.shape[0]
    group_size = lax.axis_size("expert")
    capacity = min(tok_rows, 2 * tok_rows * top_count // expert_count)
    slot_total = expert_count * capacity
    buffer_shape = (group_size, local_count, capacity, model_width)
    logits = jnp.dot(tokens, router_weight, preferred_element_type=jnp.float32)
    exp_logits = jnp.exp(logits)
    probability = exp_logits / jnp.sum(exp_logits, axis=1, keepdims=True)
    chosen = (
        routes[:, :, None] == jnp.arange(expert_count, dtype=jnp.int32)[None, None, :]
    ).astype(jnp.int32)
    chosen_float = chosen.astype(jnp.float32)
    selected = jnp.sum(chosen_float * probability[:, None, :], axis=2)
    sel_total = jnp.sum(selected, axis=1, keepdims=True)
    combine = selected / sel_total
    per_token = jnp.sum(chosen, axis=1)
    earlier = jnp.cumsum(per_token, axis=0) - per_token
    slot_ids = jnp.sum(chosen * earlier[:, None, :], axis=2)
    flat_slot = routes * capacity + slot_ids
    match_map = (
        flat_slot[:, :, None] == jnp.arange(slot_total, dtype=jnp.int32)[None, None, :]
    ).astype(jnp.float32)
    presence = jnp.sum(match_map, axis=1)
    weight_map = jnp.sum(match_map * combine[:, :, None], axis=1)
    send_rows = (
        jnp.einsum(
            "tr,td->rd", presence.astype(jnp.bfloat16), tokens, preferred_element_type=jnp.float32
        )
        .astype(jnp.bfloat16)
        .reshape(buffer_shape)
    )
    send_grads = (
        jnp.einsum(
            "tr,td->rd", weight_map, cotangent.astype(jnp.float32), precision=lax.Precision.HIGHEST
        )
        .astype(jnp.bfloat16)
        .reshape(buffer_shape)
    )
    arrived = lax.all_to_all(send_rows, "expert", split_axis=0, concat_axis=0, tiled=True)
    expert_out, stored = expert_forward(arrived, gate_weight, up_weight, down_weight)
    returned = lax.all_to_all(expert_out, "expert", split_axis=0, concat_axis=0, tiled=True)
    arrived_grads = lax.all_to_all(send_grads, "expert", split_axis=0, concat_axis=0, tiled=True)
    input_grad, gate_part, up_part = expert_backward(
        arrived_grads, stored, gate_weight, up_weight, down_weight
    )
    returned_grads = lax.all_to_all(input_grad, "expert", split_axis=0, concat_axis=0, tiled=True)
    hidden = stored[3]
    gate_term = jnp.einsum("sjcd,sjcf->jdf", arrived, gate_part, preferred_element_type=jnp.float32)
    up_term = jnp.einsum("sjcd,sjcf->jdf", arrived, up_part, preferred_element_type=jnp.float32)
    down_term = jnp.einsum(
        "sjcf,sjcd->jfd", hidden, arrived_grads, preferred_element_type=jnp.float32
    )
    gate_sum, up_sum, down_sum = (
        lax.psum_scatter(gate_term, "dp", scatter_dimension=1, tiled=True),
        lax.psum_scatter(up_term, "dp", scatter_dimension=1, tiled=True),
        lax.psum_scatter(down_term, "dp", scatter_dimension=2, tiled=True),
    )
    gate_grad = gate_sum.astype(jnp.bfloat16)
    up_grad = up_sum.astype(jnp.bfloat16)
    down_grad = down_sum.astype(jnp.bfloat16)
    flat_index = flat_slot.reshape(-1)
    out_sel = jnp.take(returned.reshape(slot_total, model_width), flat_index, axis=0).reshape(
        tok_rows, top_count, model_width
    )
    grad_sel = jnp.take(
        returned_grads.reshape(slot_total, model_width), flat_index, axis=0
    ).reshape(tok_rows, top_count, model_width)
    layer_out = jnp.sum(combine[:, :, None] * out_sel.astype(jnp.float32), axis=1).astype(
        jnp.bfloat16
    )
    comb_grad = jnp.einsum("tkd,td->tk", out_sel, cotangent, preferred_element_type=jnp.float32)
    sel_grad = (comb_grad - jnp.sum(combine * comb_grad, axis=1, keepdims=True)) / sel_total
    prob_grad = jnp.sum(chosen_float * sel_grad[:, :, None], axis=1)
    logit_grad = probability * (prob_grad - jnp.sum(probability * prob_grad, axis=1, keepdims=True))
    router_term = jnp.einsum(
        "td,te->de", tokens.astype(jnp.float32), logit_grad, precision=lax.Precision.HIGHEST
    )
    router_grad = lax.psum(router_term, ("dp", "expert"))
    router_back = jnp.einsum(
        "te,de->td", logit_grad, router_weight.astype(jnp.float32), precision=lax.Precision.HIGHEST
    )
    token_grad = (jnp.sum(grad_sel.astype(jnp.float32), axis=1) + router_back).astype(jnp.bfloat16)
    return (layer_out, token_grad, gate_grad, up_grad, down_grad, router_grad)


def solution(mesh):
    return jax.shard_map(
        local,
        mesh=mesh,
        in_specs=(
            P(("dp", "expert"), None),
            P(("dp", "expert"), None),
            P(("dp", "expert"), None),
            P(),
            P("expert", None, None),
            P("expert", None, None),
            P("expert", None, None),
        ),
        out_specs=(
            P(("dp", "expert"), None),
            P(("dp", "expert"), None),
            P("expert", "dp", None),
            P("expert", "dp", None),
            P("expert", None, "dp"),
            P(),
        ),
        check_vma=False,
    )
```

profile of v0, /device:TPU:0, one launch (start us, length us, event | category | flops | bytes accessed | tf_op | source)
XLA Modules:
  0.0 455.1 jit_solution(14684139448227573478)
XLA Ops:
  8.0 0.0 copy-start
  8.0 0.9 convert_reduce_fusion.2
  8.9 0.1 copy.29
  8.9 1.1 fusion.55
  10.1 0.7 fusion.48
  10.8 0.1 copy.28
  10.9 0.1 reduce_window_sum.11
  10.9 0.1 copy.31
  11.0 0.7 select_reduce_fusion.1
  11.7 0.7 multiply_add_fusion
  12.4 0.1 copy.32
  12.5 0.4 select_reduce_fusion
  12.9 4.0 convolution_convert_fusion
  16.9 7.5 %all-to-all-start.2 = ((bf16[16,1,32,2048]{3,2,1,0:T(8,128)(2,1)}), bf16[16,1,32,2048]{3,2,1,0:T(8,128)(2,1)}, u32[]{:S(2)}, u32[]{:S(2)}) async-start(bf16[16,1,32,2048]{3,2,1,0:T(8,128)(2,1)} %bitcast.170), calls=%async_computation.2 | async-start | bytes 4194304 | tf_op jit(solution)/shard_map/all_to_all | solution.py:86
  24.5 0.0 copy-done.1
  24.5 2.1 convolution_convert_fusion.1
  26.6 39.1 %all-to-all-done.2 = bf16[16,1,32,2048]{3,2,1,0:T(8,128)(2,1)} async-done(((bf16[16,1,32,2048]{3,2,1,0:T(8,128)(2,1)}), bf16[16,1,32,2048]{3,2,1,0:T(8,128)(2,1)}, u32[]{:S(2)}, u32[]{:S(2)}) %all-to-all-start.2) | async-done | bytes 2097184 | tf_op jit(solution)/shard_map/all_to_all | solution.py:86
  65.7 11.3 %all-to-all-start = ((bf16[16,1,32,2048]{3,2,1,0:T(8,128)(2,1)}), bf16[16,1,32,2048]{3,2,1,0:T(8,128)(2,1)}, u32[]{:S(2)}, u32[]{:S(2)}) async-start(bf16[16,1,32,2048]{3,2,1,0:T(8,128)(2,1)} %bitcast.169), calls=%async_computation | async-start | bytes 4194304 | tf_op jit(solution)/shard_map/all_to_all | solution.py:83
  76.9 0.0 reduce-scatter.8.cloned.1.call-start
  77.0 5.5 %fusion = f32[16,32,768]{2,1,0:T(8,128)} fusion(bf16[1,768,2048]{2,1,0:T(8,128)(2,1)} %param.15, bf16[16,1,32,2048]{3,2,1,0:T(8,128)(2,1)} %all-to-all-done.2), kind=kOutput, calls=%fused_computation.6 | convolution fusion | flops 1610612736 | bytes 6815744 | tf_op jit(solution)/shard_map/sjcd,jfd->sjcf/dot_general | solution.py:29
  82.5 35.6 %all-to-all-done = bf16[16,1,32,2048]{3,2,1,0:T(8,128)(2,1)} async-done(((bf16[16,1,32,2048]{3,2,1,0:T(8,128)(2,1)}), bf16[16,1,32,2048]{3,2,1,0:T(8,128)(2,1)}, u32[]{:S(2)}, u32[]{:S(2)}) %all-to-all-start) | async-done | bytes 2097184 | tf_op jit(solution)/shard_map/all_to_all | solution.py:83
  118.1 4.4 fusion.6
  122.5 0.0 copy-done
  122.5 0.0 copy-done.6
  122.5 5.1 %fusion.41 = (bf16[16,32,768]{2,1,0:T(8,128)(2,1)S(1)}, bf16[16,1,32,768]{3,2,0,1:T(8,128)(2,1)}, bf16[16,32,768]{2,1,0:T(8,128)(2,1)}) fusion(f32[16,32,768]{2,1,0:T(8,128)S(1)} %fusion.6, f32[16,32,768]{2,1,0:T(8,128)S(1)} %copy-done.6, bf16[1,2048,768]{2,1,0:T(8,128)(2,1)S(1)} %copy-done, bf16[16,1,32,2048]{3,2,1,0:T(8,128)(2,1)} %all-to-all-done), kind=kOutput, calls=%fused_computation.53 | convolution fusion | flops 1616510976 | bytes 10747904 | tf_op jit(solution)/shard_map/sjcd,jdf->sjcf/dot_general | solution.py:15
  127.6 0.9 copy-done.7
  128.5 6.1 %convolution_bitcast_fusion = f32[1,768,2048]{2,1,0:T(8,128)} fusion(bf16[16,32,768]{2,1,0:T(8,128)(2,1)S(1)} %get-tuple-element.13, bf16[16,1,32,2048]{3,2,1,0:T(8,128)(2,1)} %all-to-all-done.2), kind=kOutput, calls=%fused_computation.3 | convolution fusion | flops 1610612736 | bytes 9175040 | tf_op jit(solution)/shard_map/sjcf,sjcd->jfd/dot_general | solution.py:94
  134.6 0.0 reduce-scatter.8.cloned.1.call-update
  134.6 0.0 reduce-scatter.4.cloned.1.call-start
  134.7 6.3 %convolution_bitcast_fusion.2 = f32[1,2048,768]{2,1,0:T(8,128)} fusion(bf16[16,1,32,2048]{3,2,1,0:T(8,128)(2,1)} %all-to-all-done, bf16[16,1,32,768]{3,2,0,1:T(8,128)(2,1)} %get-tuple-element.14), kind=kOutput, calls=%fused_computation.5 | convolution fusion | flops 1610612736 | bytes 9175040 | tf_op jit(solution)/shard_map/sjcd,sjcf->jdf/dot_general | solution.py:92
  140.9 0.0 reduce-scatter.4.cloned.1.call-update
  141.0 0.2 reduce-scatter.6.cloned.1.call-start
  141.2 6.3 %convolution_bitcast_fusion.1 = f32[1,2048,768]{2,1,0:T(8,128)} fusion(bf16[16,32,768]{2,1,0:T(8,128)(2,1)} %get-tuple-element.15, bf16[16,1,32,2048]{3,2,1,0:T(8,128)(2,1)} %all-to-all-done), kind=kOutput, calls=%fused_computation.4 | convolution fusion | flops 1610612736 | bytes 9175040 | tf_op jit(solution)/shard_map/sjcd,sjcf->jdf/dot_general | solution.py:93
  147.5 0.0 reduce-scatter.6.cloned.1.call-update
  147.5 5.6 %fusion.17 = bf16[16,1,32,2048]{3,2,1,0:T(8,128)(2,1)} fusion(bf16[16,32,768]{2,1,0:T(8,128)(2,1)} %copy-done.7, bf16[1,768,2048]{2,1,0:T(8,128)(2,1)} %param.15), kind=kOutput, calls=%fused_computation.21 | convolution fusion | flops 1611661312 | bytes 6029312 | tf_op jit(solution)/shard_map/sjcf,jfd->sjcd/dot_general | solution.py:21
  153.1 11.6 %all-to-all-start.1 = ((bf16[16,1,32,2048]{3,2,1,0:T(8,128)(2,1)}), bf16[16,1,32,2048]{3,2,1,0:T(8,128)(2,1)}, u32[]{:S(2)}, u32[]{:S(2)}) async-start(bf16[16,1,32,2048]{3,2,1,0:T(8,128)(2,1)} %fusion.17), calls=%async_computation.1 | async-start | bytes 4194304 | tf_op jit(solution)/shard_map/all_to_all | solution.py:85
  164.7 0.0 copy-start.5
  164.8 4.0 fusion.4
  168.8 0.0 copy-done.5
  168.8 3.1 fusion.20
  171.9 34.0 %all-to-all-done.1 = bf16[16,1,32,2048]{3,2,1,0:T(8,128)(2,1)} async-done(((bf16[16,1,32,2048]{3,2,1,0:T(8,128)(2,1)}), bf16[16,1,32,2048]{3,2,1,0:T(8,128)(2,1)}, u32[]{:S(2)}, u32[]{:S(2)}) %all-to-all-start.1) | async-done | bytes 2097184 | tf_op jit(solution)/shard_map/all_to_all | solution.py:85
  205.9 11.3 %all-to-all-start.3 = ((bf16[16,1,32,2048]{3,2,1,0:T(8,128)(2,1)}), bf16[16,1,32,2048]{3,2,1,0:T(8,128)(2,1)}, u32[]{:S(2)}, u32[]{:S(2)}) async-start(bf16[16,1,32,2048]{3,2,1,0:T(8,128)(2,1)} %fusion.20), calls=%async_computation.3 | async-start | bytes 4194304 | tf_op jit(solution)/shard_map/all_to_all | solution.py:90
  217.2 0.0 all-reduce.2.cloned.1.call-start
  217.2 0.1 reshape.125
  217.4 0.0 copy-start.3
  217.4 5.3 %gather_fusion = bf16[256,2048]{1,0:T(8,128)(2,1)} fusion(bf16[512,2048]{1,0:T(8,128)(2,1)} %bitcast.22, s32[1024]{0:T(1024)S(1)} %pad_clamp_fusion), kind=kCustom, calls=%fused_computation.clone | custom fusion | bytes 2098176 | tf_op jit(solution)/shard_map/jit(_take)/gather | solution.py:106
  222.7 0.0 copy-done.3
  222.7 2.1 fusion.39
  224.8 0.1 copy.40
  224.9 33.4 %all-to-all-done.3 = bf16[16,1,32,2048]{3,2,1,0:T(8,128)(2,1)} async-done(((bf16[16,1,32,2048]{3,2,1,0:T(8,128)(2,1)}), bf16[16,1,32,2048]{3,2,1,0:T(8,128)(2,1)}, u32[]{:S(2)}, u32[]{:S(2)}) %all-to-all-start.3) | async-done | bytes 2097184 | tf_op jit(solution)/shard_map/all_to_all | solution.py:90
  258.3 5.2 %gather_fusion.1 = bf16[256,2048]{1,0:T(8,128)(2,1)} fusion(bf16[512,2048]{1,0:T(8,128)(2,1)} %bitcast.40, s32[1024]{0:T(1024)S(1)} %pad_clamp_fusion), kind=kCustom, calls=%fused_computation.1.clone | custom fusion | bytes 2098176 | tf_op jit(solution)/shard_map/jit(_take)/gather | solution.py:109
  263.6 0.0 copy-done.4
  263.6 0.9 convolution_bitcast_fusion.3
  264.5 4.0 convert_reduce_fusion
  268.5 0.0 all-reduce.2.cloned.1.call-update
  268.5 0.0 copy-done.2
  268.5 1.0 fusion.23
  269.5 3.3 convert_element_type.102
  272.7 25.2 %reduce-scatter.4.cloned.1.call-done = f32[1,1024,768]{2,1,0:T(8,128)} async-done(((f32[1,2048,768]{2,1,0:T(8,128)}), f32[1,1024,768]{2,1,0:T(8,128)}) %reduce-scatter.4.cloned.1.call-update) | async-done | bytes 3145744 | tf_op jit(solution)/shard_map/reduce_scatter | solution.py:98
  297.9 3.2 convert_element_type.100
  301.1 76.4 %reduce-scatter.6.cloned.1.call-done = f32[1,1024,768]{2,1,0:T(8,128)} async-done(((f32[1,2048,768]{2,1,0:T(8,128)}), f32[1,1024,768]{2,1,0:T(8,128)}) %reduce-scatter.6.cloned.1.call-update) | async-done | bytes 3145744 | tf_op jit(solution)/shard_map/reduce_scatter | solution.py:99
  377.6 3.2 convert_element_type.101
  380.8 65.6 %all-reduce.2.cloned.1.call-done = f32[2048,16]{0,1:T(8,128)} async-done(((f32[2048,16]{0,1:T(8,128)}), f32[2048,16]{0,1:T(8,128)}) %all-reduce.2.cloned.1.call-update) | async-done | bytes 131088 | tf_op jit(solution)/shard_map/psum | solution.py:122
  446.4 1.6 copy.44
  (16 shorter events, 0.1 us)
Async XLA Ops:
  8.0 114.5 %copy-start = (bf16[1,2048,768]{2,1,0:T(8,128)(2,1)S(1)}, bf16[1,2048,768]{2,1,0:T(8,128)(2,1)}, u32[]{:S(2)}) copy-start(bf16[1,2048,768]{2,1,0:T(8,128)(2,1)} %param.13) | copy-start | bytes 9437188
  16.9 7.6 %copy-start.1 = (bf16[32,2048]{1,0:T(8,128)(2,1)S(1)}, bf16[32,2048]{1,0:T(8,128)(2,1)}, u32[]{:S(2)}) copy-start(bf16[32,2048]{1,0:T(8,128)(2,1)} %param.9) | copy-start | bytes 393220
  16.9 48.7 %all-to-all-start.2 = ((bf16[16,1,32,2048]{3,2,1,0:T(8,128)(2,1)}), bf16[16,1,32,2048]{3,2,1,0:T(8,128)(2,1)}, u32[]{:S(2)}, u32[]{:S(2)}) async-start(bf16[16,1,32,2048]{3,2,1,0:T(8,128)(2,1)} %bitcast.170), calls=%async_computation.2 | async-start | bytes 4194304 | tf_op jit(solution)/shard_map/all_to_all | solution.py:86
  65.7 52.4 %all-to-all-start = ((bf16[16,1,32,2048]{3,2,1,0:T(8,128)(2,1)}), bf16[16,1,32,2048]{3,2,1,0:T(8,128)(2,1)}, u32[]{:S(2)}, u32[]{:S(2)}) async-start(bf16[16,1,32,2048]{3,2,1,0:T(8,128)(2,1)} %bitcast.169), calls=%async_computation | async-start | bytes 4194304 | tf_op jit(solution)/shard_map/all_to_all | solution.py:83
  76.9 192.5 %reduce-scatter.8.cloned.1.call-start = ((), (), s32[]{:S(2)}) async-start(), calls=%async_computation.9 | async-start | bytes 9437184 | tf_op jit(solution)/shard_map/reduce_scatter | solution.py:100
  118.1 4.4 copy-start.6
  127.6 0.9 copy-start.7
  134.6 163.3 %reduce-scatter.4.cloned.1.call-start = ((), (), s32[]{:S(2)}) async-start(), calls=%async_computation.7 | async-start | bytes 9437184 | tf_op jit(solution)/shard_map/reduce_scatter | solution.py:98
  141.0 236.6 %reduce-scatter.6.cloned.1.call-start = ((), (), s32[]{:S(2)}) async-start(), calls=%async_computation.8 | async-start | bytes 9437184 | tf_op jit(solution)/shard_map/reduce_scatter | solution.py:99
  153.1 52.8 %all-to-all-start.1 = ((bf16[16,1,32,2048]{3,2,1,0:T(8,128)(2,1)}), bf16[16,1,32,2048]{3,2,1,0:T(8,128)(2,1)}, u32[]{:S(2)}, u32[]{:S(2)}) async-start(bf16[16,1,32,2048]{3,2,1,0:T(8,128)(2,1)} %fusion.17), calls=%async_computation.1 | async-start | bytes 4194304 | tf_op jit(solution)/shard_map/all_to_all | solution.py:85
  164.7 4.0 copy-start.5
  205.9 52.4 %all-to-all-start.3 = ((bf16[16,1,32,2048]{3,2,1,0:T(8,128)(2,1)}), bf16[16,1,32,2048]{3,2,1,0:T(8,128)(2,1)}, u32[]{:S(2)}, u32[]{:S(2)}) async-start(bf16[16,1,32,2048]{3,2,1,0:T(8,128)(2,1)} %fusion.20), calls=%async_computation.3 | async-start | bytes 4194304 | tf_op jit(solution)/shard_map/all_to_all | solution.py:90
  217.2 229.2 %all-reduce.2.cloned.1.call-start = ((), (), s32[]{:S(2)}) async-start(), calls=%async_computation.10 | async-start | bytes 262144 | tf_op jit(solution)/shard_map/psum | solution.py:122
  217.4 5.4 %copy-start.3 = (bf16[32,2048]{1,0:T(8,128)(2,1)S(1)}, bf16[32,2048]{1,0:T(8,128)(2,1)}, u32[]{:S(2)}) copy-start(bf16[32,2048]{1,0:T(8,128)(2,1)} %param.11) | copy-start | bytes 393220
  258.3 5.2 %copy-start.4 = (s32[32,8]{0,1:T(8,128)S(1)}, s32[32,8]{0,1:T(8,128)}, u32[]{:S(2)}) copy-start(s32[32,8]{0,1:T(8,128)} %param.10) | copy-start | bytes 3076
  263.5 4.9 %copy-start.2 = (bf16[2048,16]{0,1:T(8,128)(2,1)S(1)}, bf16[2048,16]{0,1:T(8,128)(2,1)}, u32[]{:S(2)}) copy-start(bf16[2048,16]{0,1:T(8,128)(2,1)} %param.12) | copy-start | bytes 196612
Sparse Core Ops, SparseCore 0:
  134.7 83.5 reduce-scatter.7
  220.8 77.0 reduce-scatter.3
  300.2 77.2 reduce-scatter.5
Sparse Core Ops, SparseCore 1:
  268.6 177.8 all-reduce.1
where the time goes:
time: 456 us; the launch traced here: 455 us
  waiting for transfers between devices  309 us (68%)
  matrix products  57.6 us (13%)
  starting transfers between devices  42 us (9%)
  other arithmetic  17.2 us (4%)
  between operations  15.4 us (3%)
  local copies, waits for them, and re-layouts  13.5 us (3%)
    reduce_scatter x1, waiting for transfers between devices, local(): lax.psum_scatter(up_term, 'dp', scatter_dimension=1, tiled=True)  76.4 us
    psum x1, waiting for transfers between devices, local(): router_grad = lax.psum(router_term, ('dp', 'expert'))  65.6 us
    all_to_all x1, waiting for transfers between devices, local(): lax.all_to_all(send_grads, 'expert', split_axis=0, concat_axis=0, tiled=T...  39.1 us
    all_to_all x1, waiting for transfers between devices, local(): lax.all_to_all(send_rows, 'expert', split_axis=0, concat_axis=0, tiled=True)  35.6 us
    all_to_all x1, waiting for transfers between devices, local(): lax.all_to_all(expert_out, 'expert', split_axis=0, concat_axis=0, tiled=T...  34 us
    all_to_all x1, waiting for transfers between devices, local(): lax.all_to_all(input_grad, 'expert', split_axis=0, concat_axis=0, tiled=T...  33.4 us
    reduce_scatter x1, waiting for transfers between devices, local(): lax.psum_scatter(gate_term, 'dp', scatter_dimension=1, tiled=True)  25.2 us
    all_to_all x1, starting transfers between devices, local(): lax.all_to_all(expert_out, 'expert', split_axis=0, concat_axis=0, tiled=T...  11.6 us
  transfers between devices with their start and end apart: 8, of which 7 were waited for; matrix products, arithmetic and copies ran while one was open for 13% of the time, Pallas kernels for 0%

commit v1 on v0

--- a/solution.py
+++ b/solution.py
@@ -82,7 +82,19 @@
     )
     arrived = lax.all_to_all(send_rows, "expert", split_axis=0, concat_axis=0, tiled=True)
     expert_out, stored = expert_forward(arrived, gate_weight, up_weight, down_weight)
-    returned = lax.all_to_all(expert_out, "expert", split_axis=0, concat_axis=0, tiled=True)
+    ways, here = (lax.axis_size("expert"), lax.axis_index("expert"))
+    width = expert_out.shape[0] // ways
+    shape = list(expert_out.shape)
+    shape[0] = width
+    height = shape[0]
+    shape[0] = height * ways
+    full = jnp.zeros(shape, expert_out.dtype)
+    for mask in range(ways):
+        part = lax.dynamic_slice_in_dim(expert_out, (here ^ mask) * width, width, axis=0)
+        if mask:
+            part = lax.ppermute(part, "expert", [(d, d ^ mask) for d in range(ways)])
+        full = lax.dynamic_update_slice_in_dim(full, part, (here ^ mask) * height, axis=0)
+    returned = full
     arrived_grads = lax.all_to_all(send_grads, "expert", split_axis=0, concat_axis=0, tiled=True)
     input_grad, gate_part, up_part = expert_backward(
         arrived_grads, stored, gate_weight, up_weight, down_weight

time: 456 us -> 473 us (1.037)
  local copies, waits for them, and re-layouts: 13.5 us -> 33.4 us
  starting transfers between devices: 42 us -> 48.1 us
  waiting for transfers between devices: 309 us -> 303 us
    ppermute x0 -> x15, waiting for transfers between devices: none -> 76.4 us  [local(): part = lax.ppermute(part, 'expert', [(d, d ^ mask) for d in range(ways)])]
    all_to_all x1 -> x0, waiting for transfers between devices: 34 us -> none  [local(): lax.all_to_all(expert_out, 'expert', split_axis=0, concat_axis=0, tiled=T...]
    all_to_all x1, waiting for transfers between devices: 33.4 us -> 0.01 us  [local(): lax.all_to_all(input_grad, 'expert', split_axis=0, concat_axis=0, tiled=T...]
    reduce_scatter x1, waiting for transfers between devices: 25.2 us -> 0.01 us  [local(): lax.psum_scatter(gate_term, 'dp', scatter_dimension=1, tiled=True)]
    ppermute x0 -> x15, starting transfers between devices: none -> 22.8 us  [local(): part = lax.ppermute(part, 'expert', [(d, d ^ mask) for d in range(ways)])]
    psum x1, waiting for transfers between devices: 65.6 us -> 82.4 us  [local(): router_grad = lax.psum(router_term, ('dp', 'expert'))]
    dynamic_update_slice x0 -> x16, local copies, waits for them, and re-layouts: none -> 15.9 us  [local(): lax.dynamic_update_slice_in_dim(full, part, (here ^ mask) * height, axis=0)]
    all_to_all x1 -> x0, starting transfers between devices: 11.6 us -> none  [local(): lax.all_to_all(expert_out, 'expert', split_axis=0, concat_axis=0, tiled=T...]
  transfers between devices with their start and end apart: 8 -> 22, of which waited for: 7 -> 14; matrix products, arithmetic and copies ran while one was open for 13% -> 16% of each run, Pallas kernels for 0% -> 0%
where the time goes in v1:
time: 473 us; the launch traced here: 472 us
  waiting for transfers between devices  303 us (64%)
  matrix products  54 us (11%)
  starting transfers between devices  48.1 us (10%)
  local copies, waits for them, and re-layouts  33.4 us (7%)
  other arithmetic  17.5 us (4%)
  between operations  15.6 us (3%)
    psum x1, waiting for transfers between devices, local(): router_grad = lax.psum(router_term, ('dp', 'expert'))  82.4 us
    ppermute x15, waiting for transfers between devices, local(): part = lax.ppermute(part, 'expert', [(d, d ^ mask) for d in range(ways)])  76.4 us
    reduce_scatter x1, waiting for transfers between devices, local(): lax.psum_scatter(up_term, 'dp', scatter_dimension=1, tiled=True)  69.5 us
    all_to_all x1, waiting for transfers between devices, local(): lax.all_to_all(send_grads, 'expert', split_axis=0, concat_axis=0, tiled=T...  39.1 us
    all_to_all x1, waiting for transfers between devices, local(): lax.all_to_all(send_rows, 'expert', split_axis=0, concat_axis=0, tiled=True)  35.6 us
    ppermute x15, starting transfers between devices, local(): part = lax.ppermute(part, 'expert', [(d, d ^ mask) for d in range(ways)])  22.8 us
    dynamic_update_slice x16, local copies, waits for them, and re-layouts, local(): lax.dynamic_update_slice_in_dim(full, part, (here ^ mask) * height, axis=0)  15.9 us
    all_to_all x1, starting transfers between devices, local(): lax.all_to_all(send_rows, 'expert', split_axis=0, concat_axis=0, tiled=True)  11.3 us
  transfers between devices with their start and end apart: 22, of which 14 were waited for; matrix products, arithmetic and copies ran while one was open for 16% of the time, Pallas kernels for 0%

profile of v1, /device:TPU:0, one launch (start us, length us, event | category | flops | bytes accessed | tf_op | source)
XLA Modules:
  0.0 471.7 jit_solution(15565669161071847590)
XLA Ops:
  8.0 0.9 convert_reduce_fusion.2
  8.9 1.1 fusion.52
  10.1 0.7 fusion.45
  11.0 0.7 select_reduce_fusion.1
  11.7 0.7 multiply_add_fusion
  12.9 4.1 convolution_convert_fusion
  17.0 7.5 %all-to-all-start.1 = ((bf16[16,1,32,2048]{3,2,1,0:T(8,128)(2,1)}), bf16[16,1,32,2048]{3,2,1,0:T(8,128)(2,1)}, u32[]{:S(2)}, u32[]{:S(2)}) async-start(bf16[16,1,32,2048]{3,2,1,0:T(8,128)(2,1)} %bitcast.256), calls=%async_computation.1 | async-start | bytes 4194304 | tf_op jit(solution)/shard_map/all_to_all | solution.py:98
  24.5 2.1 convolution_convert_fusion.1
  26.6 39.1 %all-to-all-done.1 = bf16[16,1,32,2048]{3,2,1,0:T(8,128)(2,1)} async-done(((bf16[16,1,32,2048]{3,2,1,0:T(8,128)(2,1)}), bf16[16,1,32,2048]{3,2,1,0:T(8,128)(2,1)}, u32[]{:S(2)}, u32[]{:S(2)}) %all-to-all-start.1) | async-done | bytes 2097184 | tf_op jit(solution)/shard_map/all_to_all | solution.py:98
  65.7 11.3 %all-to-all-start = ((bf16[16,1,32,2048]{3,2,1,0:T(8,128)(2,1)}), bf16[16,1,32,2048]{3,2,1,0:T(8,128)(2,1)}, u32[]{:S(2)}, u32[]{:S(2)}) async-start(bf16[16,1,32,2048]{3,2,1,0:T(8,128)(2,1)} %bitcast.255), calls=%async_computation | async-start | bytes 4194304 | tf_op jit(solution)/shard_map/all_to_all | solution.py:83
  77.0 5.5 %fusion = f32[16,32,768]{2,1,0:T(8,128)} fusion(bf16[1,768,2048]{2,1,0:T(8,128)(2,1)} %param.15, bf16[16,1,32,2048]{3,2,1,0:T(8,128)(2,1)} %all-to-all-done.1), kind=kOutput, calls=%fused_computation.6 | convolution fusion | flops 1610612736 | bytes 6815744 | tf_op jit(solution)/shard_map/sjcd,jfd->sjcf/dot_general | solution.py:29
  82.5 35.6 %all-to-all-done = bf16[16,1,32,2048]{3,2,1,0:T(8,128)(2,1)} async-done(((bf16[16,1,32,2048]{3,2,1,0:T(8,128)(2,1)}), bf16[16,1,32,2048]{3,2,1,0:T(8,128)(2,1)}, u32[]{:S(2)}, u32[]{:S(2)}) %all-to-all-start) | async-done | bytes 2097184 | tf_op jit(solution)/shard_map/all_to_all | solution.py:83
  118.1 4.4 fusion.6
  122.6 5.1 %fusion.38 = (bf16[16,32,768]{2,1,0:T(8,128)(2,1)S(1)}, bf16[16,1,32,768]{3,2,0,1:T(8,128)(2,1)}, bf16[16,32,768]{2,1,0:T(8,128)(2,1)}) fusion(f32[16,32,768]{2,1,0:T(8,128)S(1)} %fusion.6, f32[16,32,768]{2,1,0:T(8,128)S(1)} %copy-done.20, bf16[1,2048,768]{2,1,0:T(8,128)(2,1)S(1)} %copy-done, bf16[16,1,32,2048]{3,2,1,0:T(8,128)(2,1)} %all-to-all-done), kind=kOutput, calls=%fused_computation.52 | convolution fusion | flops 1616510976 | bytes 10747904 | tf_op jit(solution)/shard_map/sjcd,jdf->sjcf/dot_general | solution.py:15
  127.7 0.9 copy-done.19
  128.5 6.1 %convolution_bitcast_fusion = f32[1,768,2048]{2,1,0:T(8,128)} fusion(bf16[16,32,768]{2,1,0:T(8,128)(2,1)S(1)} %get-tuple-element.13, bf16[16,1,32,2048]{3,2,1,0:T(8,128)(2,1)} %all-to-all-done.1), kind=kOutput, calls=%fused_computation.3 | convolution fusion | flops 1610612736 | bytes 9175040 | tf_op jit(solution)/shard_map/sjcf,sjcd->jfd/dot_general | solution.py:106
  134.7 6.2 %convolution_bitcast_fusion.2 = f32[1,2048,768]{2,1,0:T(8,128)} fusion(bf16[16,1,32,2048]{3,2,1,0:T(8,128)(2,1)} %all-to-all-done, bf16[16,1,32,768]{3,2,0,1:T(8,128)(2,1)} %get-tuple-element.14), kind=kOutput, calls=%fused_computation.5 | convolution fusion | flops 1610612736 | bytes 9175040 | tf_op jit(solution)/shard_map/sjcd,sjcf->jdf/dot_general | solution.py:104
  141.2 6.3 %convolution_bitcast_fusion.1 = f32[1,2048,768]{2,1,0:T(8,128)} fusion(bf16[16,32,768]{2,1,0:T(8,128)(2,1)} %get-tuple-element.15, bf16[16,1,32,2048]{3,2,1,0:T(8,128)(2,1)} %all-to-all-done), kind=kOutput, calls=%fused_computation.4 | convolution fusion | flops 1610612736 | bytes 9175040 | tf_op jit(solution)/shard_map/sjcd,sjcf->jdf/dot_general | solution.py:105
  147.8 4.2 fusion.12
  152.0 1.3 copy-done.1
  153.3 1.2 dynamic-slice_bitcast_fusion
  154.5 10.2 %collective-permute-start.14 = (bf16[1,1,32,2048]{3,2,0,1:T(8,128)(2,1)S(1)}, bf16[1,1,32,2048]{3,2,0,1:T(8,128)(2,1)}, u32[]{:S(2)}, u32[]{:S(2)}) collective-permute-start(bf16[1,1,32,2048]{3,2,0,1:T(8,128)(2,1)S(1)} %get-tuple-element.16), channel_id=1, source_target_pairs={{0,15},{1,14},{2,13},{3,12},{4,11},{5,10},{6,9},{7,8},{8,7},{9,6},... | collective-permute-start | bytes 393224 | tf_op jit(solution)/shard_map/ppermute | solution.py:95
  164.9 3.5 collective-permute-start.11
  168.5 1.8 fusion.4
  170.4 3.1 fusion.17
  173.5 6.0 %all-to-all-start.2 = ((bf16[16,1,32,2048]{3,2,1,0:T(8,128)(2,1)}), bf16[16,1,32,2048]{3,2,1,0:T(8,128)(2,1)}, u32[]{:S(2)}, u32[]{:S(2)}) async-start(bf16[16,1,32,2048]{3,2,1,0:T(8,128)(2,1)} %fusion.17), calls=%async_computation.2 | async-start | bytes 4194304 | tf_op jit(solution)/shard_map/all_to_all | solution.py:102
  179.9 1.6 broadcast_in_dim.8
  181.5 1.5 bitcast_dynamic-update-slice_fusion
  183.0 1.9 collective-permute-start.1
  184.9 1.6 constant_dynamic-update-slice_fusion.13
  186.5 13.4 %collective-permute-done.1 = bf16[1,1,32,2048]{3,2,0,1:T(8,128)(2,1)S(1)} collective-permute-done((bf16[1,1,32,2048]{3,2,0,1:T(8,128)(2,1)S(1)}, bf16[1,1,32,2048]{3,2,0,1:T(8,128)(2,1)S(1)}, u32[]{:S(2)}, u32[]{:S(2)}) %collective-permute-start.1) | collective-permute-done | bytes 131104 | tf_op jit(solution)/shard_map/ppermute | solution.py:95
  200.5 4.9 %collective-permute-done.2 = bf16[1,1,32,2048]{3,2,0,1:T(8,128)(2,1)S(1)} collective-permute-done((bf16[1,1,32,2048]{3,2,0,1:T(8,128)(2,1)S(1)}, bf16[1,1,32,2048]{3,2,0,1:T(8,128)(2,1)S(1)}, u32[]{:S(2)}, u32[]{:S(2)}) %collective-permute-start.2) | collective-permute-done | bytes 131104 | tf_op jit(solution)/shard_map/ppermute | solution.py:95
  205.4 0.7 constant_dynamic-update-slice_fusion.11
  206.0 11.2 %collective-permute-done.3 = bf16[1,1,32,2048]{3,2,0,1:T(8,128)(2,1)S(1)} collective-permute-done((bf16[1,1,32,2048]{3,2,0,1:T(8,128)(2,1)S(1)}, bf16[1,1,32,2048]{3,2,0,1:T(8,128)(2,1)S(1)}, u32[]{:S(2)}, u32[]{:S(2)}) %collective-permute-start.3) | collective-permute-done | bytes 131104 | tf_op jit(solution)/shard_map/ppermute | solution.py:95
  217.3 2.0 collective-permute-start.4
  219.3 0.7 constant_dynamic-update-slice_fusion.10
  219.9 7.8 %collective-permute-done.4 = bf16[1,1,32,2048]{3,2,0,1:T(8,128)(2,1)S(1)} collective-permute-done((bf16[1,1,32,2048]{3,2,0,1:T(8,128)(2,1)S(1)}, bf16[1,1,32,2048]{3,2,0,1:T(8,128)(2,1)S(1)}, u32[]{:S(2)}, u32[]{:S(2)}) %collective-permute-start.4) | collective-permute-done | bytes 131104 | tf_op jit(solution)/shard_map/ppermute | solution.py:95
  227.7 1.1 collective-permute-start.5
  229.5 4.7 collective-permute-done.5
  234.8 5.5 %collective-permute-done.6 = bf16[1,1,32,2048]{3,2,0,1:T(8,128)(2,1)S(1)} collective-permute-done((bf16[1,1,32,2048]{3,2,0,1:T(8,128)(2,1)S(1)}, bf16[1,1,32,2048]{3,2,0,1:T(8,128)(2,1)S(1)}, u32[]{:S(2)}, u32[]{:S(2)}) %collective-permute-start.6) | collective-permute-done | bytes 131104 | tf_op jit(solution)/shard_map/ppermute | solution.py:95
  240.3 3.8 collective-permute-start.7
  244.7 5.3 %collective-permute-done.7 = bf16[1,1,32,2048]{3,2,0,1:T(8,128)(2,1)S(1)} collective-permute-done((bf16[1,1,32,2048]{3,2,0,1:T(8,128)(2,1)S(1)}, bf16[1,1,32,2048]{3,2,0,1:T(8,128)(2,1)S(1)}, u32[]{:S(2)}, u32[]{:S(2)}) %collective-permute-start.7) | collective-permute-done | bytes 131104 | tf_op jit(solution)/shard_map/ppermute | solution.py:95
  250.7 7.2 %collective-permute-done.8 = bf16[1,1,32,2048]{3,2,0,1:T(8,128)(2,1)S(1)} collective-permute-done((bf16[1,1,32,2048]{3,2,0,1:T(8,128)(2,1)S(1)}, bf16[1,1,32,2048]{3,2,0,1:T(8,128)(2,1)S(1)}, u32[]{:S(2)}, u32[]{:S(2)}) %collective-permute-start.8) | collective-permute-done | bytes 131104 | tf_op jit(solution)/shard_map/ppermute | solution.py:95
  257.9 0.7 constant_dynamic-update-slice_fusion.5
  258.6 8.4 %collective-permute-done.9 = bf16[1,1,32,2048]{3,2,0,1:T(8,128)(2,1)S(1)} collective-permute-done((bf16[1,1,32,2048]{3,2,0,1:T(8,128)(2,1)S(1)}, bf16[1,1,32,2048]{3,2,0,1:T(8,128)(2,1)S(1)}, u32[]{:S(2)}, u32[]{:S(2)}) %collective-permute-start.9) | collective-permute-done | bytes 131104 | tf_op jit(solution)/shard_map/ppermute | solution.py:95
  267.0 0.7 constant_dynamic-update-slice_fusion.4
  267.7 8.0 %collective-permute-done.10 = bf16[1,1,32,2048]{3,2,0,1:T(8,128)(2,1)S(1)} collective-permute-done((bf16[1,1,32,2048]{3,2,0,1:T(8,128)(2,1)S(1)}, bf16[1,1,32,2048]{3,2,0,1:T(8,128)(2,1)S(1)}, u32[]{:S(2)}, u32[]{:S(2)}) %collective-permute-start.10) | collective-permute-done | bytes 131104 | tf_op jit(solution)/shard_map/ppermute | solution.py:95
  275.7 0.7 constant_dynamic-update-slice_fusion.3
  276.4 1.6 constant_dynamic-update-slice_fusion.2
  277.9 1.6 constant_dynamic-update-slice_fusion.1
  279.5 1.6 constant_dynamic-update-slice_fusion
  281.1 1.6 constant_dynamic-update-slice_fusion.14
  282.6 5.2 %gather_fusion = bf16[256,2048]{1,0:T(8,128)(2,1)} fusion(bf16[512,2048]{1,0:T(8,128)(2,1)} %bitcast.66, s32[1024]{0:T(1024)S(1)} %pad_clamp_fusion), kind=kCustom, calls=%fused_computation.clone | custom fusion | bytes 2098176 | tf_op jit(solution)/shard_map/jit(_take)/gather | solution.py:118
  287.9 2.2 fusion.36
  290.2 0.9 convolution_bitcast_fusion.3
  291.1 5.2 %gather_fusion.1 = bf16[256,2048]{1,0:T(8,128)(2,1)} fusion(bf16[512,2048]{1,0:T(8,128)(2,1)} %bitcast.84, s32[1024]{0:T(1024)S(1)} %pad_clamp_fusion), kind=kCustom, calls=%fused_computation.1.clone | custom fusion | bytes 2098176 | tf_op jit(solution)/shard_map/jit(_take)/gather | solution.py:121
  296.3 4.0 convert_reduce_fusion
  300.3 1.0 fusion.20
  301.2 3.3 convert_element_type.93
  304.5 3.5 convert_element_type.91
  308.0 69.5 %reduce-scatter.6.cloned.1.call-done = f32[1,1024,768]{2,1,0:T(8,128)} async-done(((f32[1,2048,768]{2,1,0:T(8,128)}), f32[1,1024,768]{2,1,0:T(8,128)}) %reduce-scatter.6.cloned.1.call-update) | async-done | bytes 3145744 | tf_op jit(solution)/shard_map/reduce_scatter | solution.py:111
  377.5 3.2 convert_element_type.92
  380.7 82.4 %all-reduce.2.cloned.1.call-done = f32[2048,16]{0,1:T(8,128)} async-done(((f32[2048,16]{0,1:T(8,128)}), f32[2048,16]{0,1:T(8,128)}) %all-reduce.2.cloned.1.call-update) | async-done | bytes 131088 | tf_op jit(solution)/shard_map/psum | solution.py:134
  463.0 1.6 copy.58
  (88 shorter events, 5.4 us)
Async XLA Ops:
  8.0 114.5 %copy-start = (bf16[1,2048,768]{2,1,0:T(8,128)(2,1)S(1)}, bf16[1,2048,768]{2,1,0:T(8,128)(2,1)}, u32[]{:S(2)}) copy-start(bf16[1,2048,768]{2,1,0:T(8,128)(2,1)} %param.13) | copy-start | bytes 9437188
  17.0 7.6 %copy-start.2 = (bf16[32,2048]{1,0:T(8,128)(2,1)S(1)}, bf16[32,2048]{1,0:T(8,128)(2,1)}, u32[]{:S(2)}) copy-start(bf16[32,2048]{1,0:T(8,128)(2,1)} %param.9) | copy-start | bytes 393220
  17.0 48.7 %all-to-all-start.1 = ((bf16[16,1,32,2048]{3,2,1,0:T(8,128)(2,1)}), bf16[16,1,32,2048]{3,2,1,0:T(8,128)(2,1)}, u32[]{:S(2)}, u32[]{:S(2)}) async-start(bf16[16,1,32,2048]{3,2,1,0:T(8,128)(2,1)} %bitcast.256), calls=%async_computation.1 | async-start | bytes 4194304 | tf_op jit(solution)/shard_map/all_to_all | solution.py:98
  65.7 52.4 %all-to-all-start = ((bf16[16,1,32,2048]{3,2,1,0:T(8,128)(2,1)}), bf16[16,1,32,2048]{3,2,1,0:T(8,128)(2,1)}, u32[]{:S(2)}, u32[]{:S(2)}) async-start(bf16[16,1,32,2048]{3,2,1,0:T(8,128)(2,1)} %bitcast.255), calls=%async_computation | async-start | bytes 4194304 | tf_op jit(solution)/shard_map/all_to_all | solution.py:83
  77.0 224.3 %reduce-scatter.8.cloned.1.call-start = ((), (), s32[]{:S(2)}) async-start(), calls=%async_computation.8 | async-start | bytes 9437184 | tf_op jit(solution)/shard_map/reduce_scatter | solution.py:112
  118.1 4.4 copy-start.20
  127.6 0.9 copy-start.19
  134.6 169.9 %reduce-scatter.4.cloned.1.call-start = ((), (), s32[]{:S(2)}) async-start(), calls=%async_computation.6 | async-start | bytes 9437184 | tf_op jit(solution)/shard_map/reduce_scatter | solution.py:110
  141.0 236.5 %reduce-scatter.6.cloned.1.call-start = ((), (), s32[]{:S(2)}) async-start(), calls=%async_computation.7 | async-start | bytes 9437184 | tf_op jit(solution)/shard_map/reduce_scatter | solution.py:111
  152.0 1.3 copy-start.1
  153.3 15.2 %copy-start.16 = (bf16[1,2048,768]{2,1,0:T(8,128)(2,1)S(1)}, bf16[1,2048,768]{2,1,0:T(8,128)(2,1)}, u32[]{:S(2)}) copy-start(bf16[1,2048,768]{2,1,0:T(8,128)(2,1)} %param.14) | copy-start | bytes 9437188
  153.3 15.2 %copy-start.18 = (bf16[16,32,768]{2,1,0:T(8,128)(2,1)S(1)}, bf16[16,32,768]{2,1,0:T(8,128)(2,1)}, u32[]{:S(2)}) copy-start(bf16[16,32,768]{2,1,0:T(8,128)(2,1)} %get-tuple-element.15) | copy-start | bytes 2359300
  154.5 126.5 %collective-permute-start.14 = (bf16[1,1,32,2048]{3,2,0,1:T(8,128)(2,1)S(1)}, bf16[1,1,32,2048]{3,2,0,1:T(8,128)(2,1)}, u32[]{:S(2)}, u32[]{:S(2)}) collective-permute-start(bf16[1,1,32,2048]{3,2,0,1:T(8,128)(2,1)S(1)} %get-tuple-element.16), channel_id=1, source_target_pairs={{0,15},{1,14},{2,13},{3,12},{4,11},{5,10},{6,9},{7,8},{8,7},{9,6},... | collective-permute-start | bytes 393224 | tf_op jit(solution)/shard_map/ppermute | solution.py:95
  164.7 114.8 %collective-permute-start.13 = (bf16[1,1,32,2048]{3,2,0,1:T(8,128)(2,1)}, bf16[1,1,32,2048]{3,2,0,1:T(8,128)(2,1)}, u32[]{:S(2)}, u32[]{:S(2)}) collective-permute-start(bf16[1,1,32,2048]{3,2,0,1:T(8,128)(2,1)} %get-tuple-element.17), channel_id=1, source_target_pairs={{0,14},{1,15},{2,12},{3,13},{4,10},{5,11},{6,8},{7,9},{8,6},{9,7},... | collective-permute-start | bytes 393224 | tf_op jit(solution)/shard_map/ppermute | solution.py:95
  164.9 113.1 %collective-permute-start.12 = (bf16[1,1,32,2048]{3,2,0,1:T(8,128)(2,1)}, bf16[1,1,32,2048]{3,2,0,1:T(8,128)(2,1)}, u32[]{:S(2)}, u32[]{:S(2)}) collective-permute-start(bf16[1,1,32,2048]{3,2,0,1:T(8,128)(2,1)} %get-tuple-element.18), channel_id=1, source_target_pairs={{0,13},{1,12},{2,15},{3,14},{4,9},{5,8},{6,11},{7,10},{8,5},{9,4},... | collective-permute-start | bytes 393224 | tf_op jit(solution)/shard_map/ppermute | solution.py:95
  164.9 111.5 %collective-permute-start.11 = (bf16[1,1,32,2048]{3,2,0,1:T(8,128)(2,1)}, bf16[1,1,32,2048]{3,2,0,1:T(8,128)(2,1)}, u32[]{:S(2)}, u32[]{:S(2)}) collective-permute-start(bf16[1,1,32,2048]{3,2,0,1:T(8,128)(2,1)} %get-tuple-element.19), channel_id=1, source_target_pairs={{0,12},{1,13},{2,14},{3,15},{4,8},{5,9},{6,10},{7,11},{8,4},{9,5},... | collective-permute-start | bytes 393224 | tf_op jit(solution)/shard_map/ppermute | solution.py:95
  168.4 2.0 copy-start.17
  168.4 14.6 %collective-permute-start = (bf16[1,1,32,2048]{3,2,0,1:T(8,128)(2,1)}, bf16[1,1,32,2048]{3,2,0,1:T(8,128)(2,1)}, u32[]{:S(2)}, u32[]{:S(2)}) collective-permute-start(bf16[1,1,32,2048]{3,2,0,1:T(8,128)(2,1)} %get-tuple-element.30), channel_id=1, source_target_pairs={{0,1},{1,0},{2,3},{3,2},{4,5},{5,4},{6,7},{7,6},{8,9},{9,8},{10,11... | collective-permute-start | bytes 393224 | tf_op jit(solution)/shard_map/ppermute | solution.py:95
  173.5 117.6 %all-to-all-start.2 = ((bf16[16,1,32,2048]{3,2,1,0:T(8,128)(2,1)}), bf16[16,1,32,2048]{3,2,1,0:T(8,128)(2,1)}, u32[]{:S(2)}, u32[]{:S(2)}) async-start(bf16[16,1,32,2048]{3,2,1,0:T(8,128)(2,1)} %fusion.17), calls=%async_computation.2 | async-start | bytes 4194304 | tf_op jit(solution)/shard_map/all_to_all | solution.py:102
  179.5 283.5 %all-reduce.2.cloned.1.call-start = ((), (), s32[]{:S(2)}) async-start(), calls=%async_computation.9 | async-start | bytes 262144 | tf_op jit(solution)/shard_map/psum | solution.py:134
  179.8 3.2 copy-start.14
  179.8 20.0 %copy-start.13 = (bf16[1,1,32,2048]{3,2,0,1:T(8,128)(2,1)S(1)}, bf16[1,1,32,2048]{3,2,0,1:T(8,128)(2,1)}, u32[]{:S(2)}) copy-start(bf16[1,1,32,2048]{3,2,0,1:T(8,128)(2,1)} %get-tuple-element.28) | copy-start | bytes 393220
  179.8 25.6 %copy-start.12 = (bf16[1,1,32,2048]{3,2,0,1:T(8,128)(2,1)S(1)}, bf16[1,1,32,2048]{3,2,0,1:T(8,128)(2,1)}, u32[]{:S(2)}) copy-start(bf16[1,1,32,2048]{3,2,0,1:T(8,128)(2,1)} %get-tuple-element.27) | copy-start | bytes 393220
  179.8 37.5 %copy-start.11 = (bf16[1,1,32,2048]{3,2,0,1:T(8,128)(2,1)S(1)}, bf16[1,1,32,2048]{3,2,0,1:T(8,128)(2,1)}, u32[]{:S(2)}) copy-start(bf16[1,1,32,2048]{3,2,0,1:T(8,128)(2,1)} %get-tuple-element.26) | copy-start | bytes 393220
  179.8 47.9 %copy-start.10 = (bf16[1,1,32,2048]{3,2,0,1:T(8,128)(2,1)S(1)}, bf16[1,1,32,2048]{3,2,0,1:T(8,128)(2,1)}, u32[]{:S(2)}) copy-start(bf16[1,1,32,2048]{3,2,0,1:T(8,128)(2,1)} %get-tuple-element.25) | copy-start | bytes 393220
  179.8 54.3 %copy-start.9 = (bf16[1,1,32,2048]{3,2,0,1:T(8,128)(2,1)S(1)}, bf16[1,1,32,2048]{3,2,0,1:T(8,128)(2,1)}, u32[]{:S(2)}) copy-start(bf16[1,1,32,2048]{3,2,0,1:T(8,128)(2,1)} %get-tuple-element.24) | copy-start | bytes 393220
  179.8 60.4 %copy-start.8 = (bf16[1,1,32,2048]{3,2,0,1:T(8,128)(2,1)S(1)}, bf16[1,1,32,2048]{3,2,0,1:T(8,128)(2,1)}, u32[]{:S(2)}) copy-start(bf16[1,1,32,2048]{3,2,0,1:T(8,128)(2,1)} %get-tuple-element.23) | copy-start | bytes 393220
  179.9 70.2 %copy-start.7 = (bf16[1,1,32,2048]{3,2,0,1:T(8,128)(2,1)S(1)}, bf16[1,1,32,2048]{3,2,0,1:T(8,128)(2,1)}, u32[]{:S(2)}) copy-start(bf16[1,1,32,2048]{3,2,0,1:T(8,128)(2,1)} %get-tuple-element.22) | copy-start | bytes 393220
  179.9 78.1 %copy-start.6 = (bf16[1,1,32,2048]{3,2,0,1:T(8,128)(2,1)S(1)}, bf16[1,1,32,2048]{3,2,0,1:T(8,128)(2,1)}, u32[]{:S(2)}) copy-start(bf16[1,1,32,2048]{3,2,0,1:T(8,128)(2,1)} %get-tuple-element.21) | copy-start | bytes 393220
  179.9 87.2 %copy-start.5 = (bf16[1,1,32,2048]{3,2,0,1:T(8,128)(2,1)S(1)}, bf16[1,1,32,2048]{3,2,0,1:T(8,128)(2,1)}, u32[]{:S(2)}) copy-start(bf16[1,1,32,2048]{3,2,0,1:T(8,128)(2,1)} %get-tuple-element.20) | copy-start | bytes 393220
  183.0 16.8 %collective-permute-start.1 = (bf16[1,1,32,2048]{3,2,0,1:T(8,128)(2,1)S(1)}, bf16[1,1,32,2048]{3,2,0,1:T(8,128)(2,1)S(1)}, u32[]{:S(2)}, u32[]{:S(2)}) collective-permute-start(bf16[1,1,32,2048]{3,2,0,1:T(8,128)(2,1)S(1)} %copy-done.14), channel_id=1, source_target_pairs={{0,2},{1,3},{2,0},{3,1},{4,6},{5,7},{6,4},{7,5},{8,10},{9,11},{10,... | collective-permute-start | bytes 393224 | tf_op jit(solution)/shard_map/ppermute | solution.py:95
  199.8 5.6 %collective-permute-start.2 = (bf16[1,1,32,2048]{3,2,0,1:T(8,128)(2,1)S(1)}, bf16[1,1,32,2048]{3,2,0,1:T(8,128)(2,1)S(1)}, u32[]{:S(2)}, u32[]{:S(2)}) collective-permute-start(bf16[1,1,32,2048]{3,2,0,1:T(8,128)(2,1)S(1)} %copy-done.13), channel_id=1, source_target_pairs={{0,3},{1,2},{2,1},{3,0},{4,7},{5,6},{6,5},{7,4},{8,11},{9,10},{10,... | collective-permute-start | bytes 393224 | tf_op jit(solution)/shard_map/ppermute | solution.py:95
  205.4 11.9 %collective-permute-start.3 = (bf16[1,1,32,2048]{3,2,0,1:T(8,128)(2,1)S(1)}, bf16[1,1,32,2048]{3,2,0,1:T(8,128)(2,1)S(1)}, u32[]{:S(2)}, u32[]{:S(2)}) collective-permute-start(bf16[1,1,32,2048]{3,2,0,1:T(8,128)(2,1)S(1)} %copy-done.12), channel_id=1, source_target_pairs={{0,4},{1,5},{2,6},{3,7},{4,0},{5,1},{6,2},{7,3},{8,12},{9,13},{10,... | collective-permute-start | bytes 393224 | tf_op jit(solution)/shard_map/ppermute | solution.py:95
  217.3 10.4 %collective-permute-start.4 = (bf16[1,1,32,2048]{3,2,0,1:T(8,128)(2,1)S(1)}, bf16[1,1,32,2048]{3,2,0,1:T(8,128)(2,1)S(1)}, u32[]{:S(2)}, u32[]{:S(2)}) collective-permute-start(bf16[1,1,32,2048]{3,2,0,1:T(8,128)(2,1)S(1)} %copy-done.11), channel_id=1, source_target_pairs={{0,5},{1,4},{2,7},{3,6},{4,1},{5,0},{6,3},{7,2},{8,13},{9,12},{10,... | collective-permute-start | bytes 393224 | tf_op jit(solution)/shard_map/ppermute | solution.py:95
  227.7 6.4 %collective-permute-start.5 = (bf16[1,1,32,2048]{3,2,0,1:T(8,128)(2,1)S(1)}, bf16[1,1,32,2048]{3,2,0,1:T(8,128)(2,1)S(1)}, u32[]{:S(2)}, u32[]{:S(2)}) collective-permute-start(bf16[1,1,32,2048]{3,2,0,1:T(8,128)(2,1)S(1)} %copy-done.10), channel_id=1, source_target_pairs={{0,6},{1,7},{2,4},{3,5},{4,2},{5,3},{6,0},{7,1},{8,14},{9,15},{10,... | collective-permute-start | bytes 393224 | tf_op jit(solution)/shard_map/ppermute | solution.py:95
  234.1 6.2 %collective-permute-start.6 = (bf16[1,1,32,2048]{3,2,0,1:T(8,128)(2,1)S(1)}, bf16[1,1,32,2048]{3,2,0,1:T(8,128)(2,1)S(1)}, u32[]{:S(2)}, u32[]{:S(2)}) collective-permute-start(bf16[1,1,32,2048]{3,2,0,1:T(8,128)(2,1)S(1)} %copy-done.9), channel_id=1, source_target_pairs={{0,7},{1,6},{2,5},{3,4},{4,3},{5,2},{6,1},{7,0},{8,15},{9,14},{10,... | collective-permute-start | bytes 393224 | tf_op jit(solution)/shard_map/ppermute | solution.py:95
  240.3 9.8 %collective-permute-start.7 = (bf16[1,1,32,2048]{3,2,0,1:T(8,128)(2,1)S(1)}, bf16[1,1,32,2048]{3,2,0,1:T(8,128)(2,1)S(1)}, u32[]{:S(2)}, u32[]{:S(2)}) collective-permute-start(bf16[1,1,32,2048]{3,2,0,1:T(8,128)(2,1)S(1)} %copy-done.8), channel_id=1, source_target_pairs={{0,8},{1,9},{2,10},{3,11},{4,12},{5,13},{6,14},{7,15},{8,0},{9,1},... | collective-permute-start | bytes 393224 | tf_op jit(solution)/shard_map/ppermute | solution.py:95
  250.0 7.9 %collective-permute-start.8 = (bf16[1,1,32,2048]{3,2,0,1:T(8,128)(2,1)S(1)}, bf16[1,1,32,2048]{3,2,0,1:T(8,128)(2,1)S(1)}, u32[]{:S(2)}, u32[]{:S(2)}) collective-permute-start(bf16[1,1,32,2048]{3,2,0,1:T(8,128)(2,1)S(1)} %copy-done.7), channel_id=1, source_target_pairs={{0,9},{1,8},{2,11},{3,10},{4,13},{5,12},{6,15},{7,14},{8,1},{9,0},... | collective-permute-start | bytes 393224 | tf_op jit(solution)/shard_map/ppermute | solution.py:95
  257.9 9.1 %collective-permute-start.9 = (bf16[1,1,32,2048]{3,2,0,1:T(8,128)(2,1)S(1)}, bf16[1,1,32,2048]{3,2,0,1:T(8,128)(2,1)S(1)}, u32[]{:S(2)}, u32[]{:S(2)}) collective-permute-start(bf16[1,1,32,2048]{3,2,0,1:T(8,128)(2,1)S(1)} %copy-done.6), channel_id=1, source_target_pairs={{0,10},{1,11},{2,8},{3,9},{4,14},{5,15},{6,12},{7,13},{8,2},{9,3},... | collective-permute-start | bytes 393224 | tf_op jit(solution)/shard_map/ppermute | solution.py:95
  267.0 8.7 %collective-permute-start.10 = (bf16[1,1,32,2048]{3,2,0,1:T(8,128)(2,1)S(1)}, bf16[1,1,32,2048]{3,2,0,1:T(8,128)(2,1)S(1)}, u32[]{:S(2)}, u32[]{:S(2)}) collective-permute-start(bf16[1,1,32,2048]{3,2,0,1:T(8,128)(2,1)S(1)} %copy-done.5), channel_id=1, source_target_pairs={{0,11},{1,10},{2,9},{3,8},{4,15},{5,14},{6,13},{7,12},{8,3},{9,2},... | collective-permute-start | bytes 393224 | tf_op jit(solution)/shard_map/ppermute | solution.py:95
  282.6 5.2 %copy-start.4 = (bf16[32,2048]{1,0:T(8,128)(2,1)S(1)}, bf16[32,2048]{1,0:T(8,128)(2,1)}, u32[]{:S(2)}) copy-start(bf16[32,2048]{1,0:T(8,128)(2,1)} %param.11) | copy-start | bytes 393220
  287.9 2.3 copy-start.15
  296.3 4.0 copy-start.3
Sparse Core Ops, SparseCore 0:
  134.8 83.5 reduce-scatter.7
  220.8 77.0 reduce-scatter.3
  300.2 77.2 reduce-scatter.5
Sparse Core Ops, SparseCore 1:
  291.2 171.8 all-reduce.1
